TPU v7x, 32 devices: a whole 2x2x4 slice. The times are simulated.
32 devices in a mesh: tm: 8 (over z, core), lat: 4 (over y, x).
Axes of the slice: x: 2, y: 2, z: 4, core: 2. Of those that a mesh axis runs over, the one named last changes fastest.
Arguments:
- window_snapshots: bfloat16 [8, 64, 32, 128], P('tm', None, 'lat'), may hold values from -6 to 6
- background: bfloat16 [64, 32, 128], P(None, 'lat'), may hold values from -6 to 6
- obs_values: bfloat16 [8, 64, 1024], P('tm', None, 'lat'), may hold values from -6 to 6
- obs_index: int32 [8, 1024], P('tm', 'lat'), may hold values from 0 to 4095, as said below
- input_kernel_weight: bfloat16 [3, 3, 256, 64], replicated, may hold values from -0.25 to 0.25
- hidden_bias_vector: float32 [256], replicated, may hold values from -3 to 3
- output_pointwise_weight: bfloat16 [64, 256], replicated, may hold values from -0.375 to 0.375
Outputs:
- analysis: bfloat16 [8, 64, 32, 128], P('tm', None, 'lat')
Inputs may be any that keep to these rules, and one draw needn't show every extreme that they name: `obs_index`: entry [k, j] is a grid column counted latitude by latitude over 128 longitudes; observations s * 256 to (s + 1) * 256 - 1 lie in latitudes s * 8 to (s + 1) * 8 - 1; a column may be observed more than once.
All inputs are finite; a program needn't handle non-finite values.
Results may differ from a plain program's by a relative error of at most 0.015.
Values may be sent and summed in bfloat16 or wider, within the bound.
A program may use at most 64 MiB of HBM per device.

v0:
```python
import jax
import jax.numpy as jnp
from jax import lax
from jax.sharding import PartitionSpec as P

ITERS = 2


step_size = 0.3


def from_behind(value, axis, by):
    length = lax.axis_size(axis)
    pairs = [(i, i + by) for i in range(length) if 0 <= i + by < length]
    return lax.ppermute(value, axis, pairs)


def with_halo(cells, sides, width):
    for axis, dim in sides:
        count = lax.axis_size(axis)
        ends = count - 1
        head = lax.slice_in_dim(cells, 0, width, axis=dim)
        tail = lax.slice_in_dim(cells, cells.shape[dim] - width, cells.shape[dim], axis=dim)
        cells = jnp.concatenate(
            [
                lax.ppermute(tail, axis, [(i, (i + 1) % count) for i in range(ends)]),
                cells,
                lax.ppermute(head, axis, [((i + 1) % count, i) for i in range(ends)]),
            ],
            axis=dim,
        )
    return cells


def shift_cells(grid_field, offset):
    return jnp.roll(grid_field, offset, axis=grid_field.ndim - 1)


def advance_one_interval(
    bordered_field, input_kernel_weight, hidden_bias_vector, output_pointwise_weight
):
    height = bordered_field.shape[1] - 2
    before = hidden_bias_vector[:, None, None]
    for row_step in range(3):
        stripe = bordered_field[:, row_step : row_step + height, :]
        for col_step in range(3):
            before = before + jnp.einsum(
                "hc,clm->hlm",
                input_kernel_weight[row_step, col_step],
                shift_cells(stripe, 1 - col_step),
                preferred_element_type=jnp.float32,
            )
    active = jnp.tanh(before).astype(jnp.bfloat16)
    centre = bordered_field[:, 1 : height + 1, :].astype(jnp.float32)
    anticipated_snapshot = centre + jnp.einsum(
        "ch,hlm->clm", output_pointwise_weight, active, preferred_element_type=jnp.float32
    )
    return (anticipated_snapshot.astype(jnp.bfloat16), active)


def make_cotangent(active, dynamics_mismatch, output_pointwise_weight):
    projected = jnp.einsum(
        "ch,clm->hlm",
        output_pointwise_weight,
        dynamics_mismatch,
        preferred_element_type=jnp.float32,
    )
    squashed = active.astype(jnp.float32)
    return ((1.0 - squashed * squashed) * projected).astype(jnp.bfloat16)


def collect_rows(bordered_field, input_kernel_weight):
    height = bordered_field.shape[1] - 2
    summed = None
    for row_step in range(3):
        stripe = bordered_field[:, 2 - row_step : 2 - row_step + height, :]
        for col_step in range(3):
            product = jnp.einsum(
                "hc,hlm->clm",
                input_kernel_weight[row_step, col_step],
                shift_cells(stripe, col_step - 1),
                preferred_element_type=jnp.float32,
            )
            summed = product if summed is None else summed + product
    return summed


def misfit_map(window_snapshots, obs_values, local_index):
    windows, channels, height, columns = window_snapshots.shape
    flattened = window_snapshots.reshape(windows, channels, height * columns)

    def scatter_one(grid_field, values, column_index):
        misfit = jnp.take(grid_field, column_index, axis=1).astype(jnp.float32) - values.astype(
            jnp.float32
        )
        return jnp.zeros(grid_field.shape, jnp.float32).at[:, column_index].add(misfit)

    return jax.vmap(scatter_one)(flattened, obs_values, local_index).reshape(window_snapshots.shape)


def widened_step(
    window_snapshots,
    background,
    input_kernel_weight,
    hidden_bias_vector,
    output_pointwise_weight,
    at_start,
):
    windows, channels, height, columns = window_snapshots.shape
    earlier_snapshot = from_behind(window_snapshots[windows - 1], "tm", 1)
    stacked = jnp.concatenate([earlier_snapshot[None], window_snapshots], axis=0)
    bordered_field = with_halo(stacked, (("lat", 2),), 2)
    anticipated_snapshot, active = lax.map(
        lambda lone_snapshot: advance_one_interval(
            lone_snapshot, input_kernel_weight, hidden_bias_vector, output_pointwise_weight
        ),
        bordered_field[:windows],
    )
    current_snapshot = bordered_field[1:, :, 1 : height + 3]
    row_ids = lax.axis_index("lat") * height + jnp.arange(height + 2, dtype=jnp.int32) - 1
    inside = jnp.logical_and(row_ids >= 0, row_ids < lax.axis_size("lat") * height)
    wide_resid = (
        current_snapshot.astype(jnp.float32) - anticipated_snapshot.astype(jnp.float32)
    ).astype(jnp.bfloat16)
    wide_resid = jnp.where(inside[None, None, :, None], wide_resid, jnp.zeros_like(wide_resid))
    cotangents = lax.map(
        lambda paired: make_cotangent(paired[0], paired[1], output_pointwise_weight),
        (active, wide_resid),
    )
    spreads = lax.map(
        lambda lone_snapshot: collect_rows(lone_snapshot, input_kernel_weight), cotangents
    )
    inner_resid = wide_resid[:, :, 1 : height + 1]
    pulled = (inner_resid.astype(jnp.float32) + spreads).astype(jnp.bfloat16)
    from_next = from_behind(pulled[0], "tm", -1)
    adjoint = jnp.concatenate([pulled[1:], from_next[None]], axis=0)
    first_resid = (window_snapshots[0].astype(jnp.float32) - background.astype(jnp.float32)).astype(
        jnp.bfloat16
    )
    opening_snapshots = jnp.where(at_start, first_resid, inner_resid[0])
    dynamics_mismatch = jnp.concatenate([opening_snapshots[None], inner_resid[1:]], axis=0)
    return (dynamics_mismatch, adjoint)


def descend(
    window_snapshots,
    background,
    obs_values,
    local_index,
    input_kernel_weight,
    hidden_bias_vector,
    output_pointwise_weight,
):
    at_start = lax.axis_index("tm") == 0
    dynamics_mismatch, adjoint = widened_step(
        window_snapshots,
        background,
        input_kernel_weight,
        hidden_bias_vector,
        output_pointwise_weight,
        at_start,
    )
    innovation = misfit_map(window_snapshots, obs_values, local_index)
    gradient = dynamics_mismatch.astype(jnp.float32) - adjoint.astype(jnp.float32) + innovation
    return (window_snapshots.astype(jnp.float32) - step_size * gradient).astype(jnp.bfloat16)


def on_device(
    window_snapshots,
    background,
    obs_values,
    obs_index,
    input_kernel_weight,
    hidden_bias_vector,
    output_pointwise_weight,
):
    strip_cells = window_snapshots.shape[2] * window_snapshots.shape[3]
    local_index = obs_index - lax.axis_index("lat") * strip_cells
    for repeat in range(ITERS):
        window_snapshots = descend(
            window_snapshots,
            background,
            obs_values,
            local_index,
            input_kernel_weight,
            hidden_bias_vector,
            output_pointwise_weight,
        )
    return window_snapshots


def solution(mesh):
    placed = (
        P("tm", None, "lat", None),
        P(None, "lat", None),
        P("tm", None, "lat"),
        P("tm", "lat"),
        P(),
        P(),
        P(),
    )
    return jax.shard_map(
        on_device, mesh=mesh, in_specs=placed, out_specs=P("tm", None, "lat", None), check_vma=False
    )
```

profile of v0, /device:TPU:19, one launch (start us, length us, event | category | flops | bytes accessed | tf_op | source)
XLA Modules:
  0.0 63.9 jit_solution(2575679197545666035)
XLA Ops:
  0.0 0.9 %copy.99 = bf16[1,64,8,128]{3,1,2,0:T(8,128)(2,1)S(1)} copy(bf16[1,64,8,128]{3,2,1,0:T(8,128)(2,1)} %param.9) | data formatting | bytes 262144 | tf_op args[0]
  0.9 3.8 %collective-permute-start = (bf16[64,8,128]{2,0,1:T(8,128)(2,1)S(1)}, bf16[64,8,128]{2,0,1:T(8,128)(2,1)S(1)}, u32[]{:S(2)}, u32[]{:S(2)}) collective-permute-start(bf16[64,8,128]{2,0,1:T(8,128)(2,1)S(1)} %bitcast.259), channel_id=1, source_target_pairs={{0,4},{4,8},{8,12},{12,16},{16,20},{20,24},{24,28},{1,5},{5,9},{9,... | collective-permute-start | bytes 393224 | tf_op jit(solution)/shard_map/ppermute | solution.py:15
  4.7 0.7 %and_reduce_fusion = (pred[256]{0:T(512)(128)(4,1)S(1)}, s32[1,256]{1,0:T(1,128)S(1)}) fusion(s32[1,256]{1,0:T(1,128)} %param.12, s32[]{:T(128)S(6)} %mul.38), kind=kLoop, calls=%fused_computation.277 | loop fusion | flops 1792 | bytes 2308 | tf_op jit(solution)/shard_map/vmap(jit(_take))/and | solution.py:93
  5.4 1.1 %copy.49 = bf16[1,64,8,128]{1,3,2,0:T(8,128)(2,1)S(1)} copy(bf16[1,64,8,128]{3,2,1,0:T(8,128)(2,1)} %param.9) | data formatting | bytes 262144 | tf_op args[0]
  6.5 0.9 %copy.50 = bf16[1,64,256]{1,2,0:T(8,128)(2,1)S(1)} copy(bf16[1,64,256]{2,1,0:T(8,128)(2,1)} %param.11) | data formatting | bytes 65536 | tf_op args[2]
  7.4 3.1 %collective-permute-start.1 = (bf16[2,64,2,128]{3,1,2,0:T(8,128)(2,1)S(1)}, bf16[2,64,2,128]{3,1,2,0:T(8,128)(2,1)S(1)}, u32[]{:S(2)}, u32[]{:S(2)}) collective-permute-start(bf16[2,64,2,128]{3,1,2,0:T(8,128)(2,1)S(1)} %get-tuple-element.128), channel_id=1, source_target_pairs={{0,1},{1,2},{2,3},{4,5},{5,6},{6,7},{8,9},{9,10},{10,11},{12,13},{... | collective-permute-start | bytes 196616 | tf_op jit(solution)/shard_map/ppermute | solution.py:26
  10.6 2.2 %collective-permute-start.2 = (bf16[2,64,2,128]{3,1,2,0:T(8,128)(2,1)S(1)}, bf16[2,64,2,128]{3,1,2,0:T(8,128)(2,1)S(1)}, u32[]{:S(2)}, u32[]{:S(2)}) collective-permute-start(bf16[2,64,2,128]{3,1,2,0:T(8,128)(2,1)S(1)} %get-tuple-element.130), channel_id=1, source_target_pairs={{1,0},{2,1},{3,2},{5,4},{6,5},{7,6},{9,8},{10,9},{11,10},{13,12},{... | collective-permute-start | bytes 196616 | tf_op jit(solution)/shard_map/ppermute | solution.py:28
  12.8 3.7 %collective-permute-done.2 = bf16[2,64,2,128]{3,1,2,0:T(8,128)(2,1)S(1)} collective-permute-done((bf16[2,64,2,128]{3,1,2,0:T(8,128)(2,1)S(1)}, bf16[2,64,2,128]{3,1,2,0:T(8,128)(2,1)S(1)}, u32[]{:S(2)}, u32[]{:S(2)}) %collective-permute-start.2) | collective-permute-done | bytes 65568 | tf_op jit(solution)/shard_map/ppermute | solution.py:28
  16.5 0.3 fusion.266
  17.1 0.7 %copy-done.1 = bf16[3,3,256,64]{2,3,1,0:T(8,128)(2,1)S(1)} copy-done((bf16[3,3,256,64]{2,3,1,0:T(8,128)(2,1)S(1)}, bf16[3,3,256,64]{2,3,1,0:T(8,128)(2,1)}, u32[]{:S(2)}) %copy-start.1) | copy-done | bytes 294936
  17.8 0.5 fusion.101
  18.3 0.5 fusion.97
  18.8 0.5 fusion.105
  19.3 0.5 fusion.109
  19.8 0.5 fusion.113
  20.4 0.5 convolution_add_fusion.7
  20.9 0.4 fusion.9
  21.2 0.4 fusion.7
  21.6 0.4 fusion.18
  22.0 0.4 fusion.92
  22.4 0.4 fusion.16
  22.8 0.4 fusion.262
  23.5 0.3 fusion.38
  23.8 0.3 fusion.27
  24.1 0.3 fusion.45
  24.4 0.3 convolution_add_fusion.17
  24.7 0.3 fusion.26
  24.9 0.3 fusion.52
  25.2 0.3 convolution_add_fusion.16
  25.6 0.3 fusion.32
  25.8 3.8 %collective-permute-start.3 = (bf16[64,8,128]{2,0,1:T(8,128)(2,1)S(1)}, bf16[64,8,128]{2,0,1:T(8,128)(2,1)S(1)}, u32[]{:S(2)}, u32[]{:S(2)}) collective-permute-start(bf16[64,8,128]{2,0,1:T(8,128)(2,1)S(1)} %fusion.32), channel_id=1, source_target_pairs={{4,0},{8,4},{12,8},{16,12},{20,16},{24,20},{28,24},{5,1},{9,5},{13... | collective-permute-start | bytes 393224 | tf_op jit(solution)/shard_map/ppermute | solution.py:15
  29.7 2.8 %scatter_custom_fusion = f32[64,1024]{0,1:T(8,128)S(1)} fusion(s32[256]{0:T(256)S(1)} %bitcast.271, f32[]{:T(128)} %constant.89.clone.1, bf16[1,64,256]{1,2,0:T(8,128)(2,1)S(1)} %copy.50, pred[256]{0:T(512)(128)(4,1)S(1)} %get-tuple-element.68, bf16[]{:T(256)} %constant.58.clone.2, bf16[1,64,1024]{1,2,0:T(8,128)(2,1)S(1)} %bitcast.260, s32[256]{0:T(256)S(1)} %bitcast.268), kind=kCustom, calls=%fused_computation.120 | custom fusion | flops 81920 | bytes 591366 | tf_op jit(solution)/shard_map/vmap()/scatter-add | solution.py:96
  32.6 0.8 %collective-permute-done.3 = bf16[64,8,128]{2,0,1:T(8,128)(2,1)S(1)} collective-permute-done((bf16[64,8,128]{2,0,1:T(8,128)(2,1)S(1)}, bf16[64,8,128]{2,0,1:T(8,128)(2,1)S(1)}, u32[]{:S(2)}, u32[]{:S(2)}) %collective-permute-start.3) | collective-permute-done | bytes 131104 | tf_op jit(solution)/shard_map/ppermute | solution.py:15
  33.6 2.3 %collective-permute-start.4 = (bf16[64,8,128]{2,0,1:T(8,128)(2,1)S(1)}, bf16[64,8,128]{2,0,1:T(8,128)(2,1)S(1)}, u32[]{:S(2)}, u32[]{:S(2)}) collective-permute-start(bf16[64,8,128]{2,0,1:T(8,128)(2,1)S(1)} %bitcast.256), channel_id=1, source_target_pairs={{0,4},{4,8},{8,12},{12,16},{16,20},{20,24},{24,28},{1,5},{5,9},{9,... | collective-permute-start | bytes 393224 | tf_op jit(solution)/shard_map/ppermute | solution.py:15
  35.9 1.9 %collective-permute-done.4 = bf16[64,8,128]{2,0,1:T(8,128)(2,1)S(1)} collective-permute-done((bf16[64,8,128]{2,0,1:T(8,128)(2,1)S(1)}, bf16[64,8,128]{2,0,1:T(8,128)(2,1)S(1)}, u32[]{:S(2)}, u32[]{:S(2)}) %collective-permute-start.4) | collective-permute-done | bytes 131104 | tf_op jit(solution)/shard_map/ppermute | solution.py:15
  37.8 2.2 %collective-permute-start.5 = (bf16[2,64,2,128]{3,1,2,0:T(8,128)(2,1)S(1)}, bf16[2,64,2,128]{3,1,2,0:T(8,128)(2,1)S(1)}, u32[]{:S(2)}, u32[]{:S(2)}) collective-permute-start(bf16[2,64,2,128]{3,1,2,0:T(8,128)(2,1)S(1)} %get-tuple-element.122), channel_id=1, source_target_pairs={{0,1},{1,2},{2,3},{4,5},{5,6},{6,7},{8,9},{9,10},{10,11},{12,13},{... | collective-permute-start | bytes 196616 | tf_op jit(solution)/shard_map/ppermute | solution.py:26
  40.1 3.2 %collective-permute-start.6 = (bf16[2,64,2,128]{3,1,2,0:T(8,128)(2,1)S(1)}, bf16[2,64,2,128]{3,1,2,0:T(8,128)(2,1)S(1)}, u32[]{:S(2)}, u32[]{:S(2)}) collective-permute-start(bf16[2,64,2,128]{3,1,2,0:T(8,128)(2,1)S(1)} %get-tuple-element.123), channel_id=1, source_target_pairs={{1,0},{2,1},{3,2},{5,4},{6,5},{7,6},{9,8},{10,9},{11,10},{13,12},{... | collective-permute-start | bytes 196616 | tf_op jit(solution)/shard_map/ppermute | solution.py:28
  43.3 2.6 %collective-permute-done.6 = bf16[2,64,2,128]{3,1,2,0:T(8,128)(2,1)S(1)} collective-permute-done((bf16[2,64,2,128]{3,1,2,0:T(8,128)(2,1)S(1)}, bf16[2,64,2,128]{3,1,2,0:T(8,128)(2,1)S(1)}, u32[]{:S(2)}, u32[]{:S(2)}) %collective-permute-start.6) | collective-permute-done | bytes 65568 | tf_op jit(solution)/shard_map/ppermute | solution.py:28
  46.0 0.3 fusion.264
  46.6 0.5 convolution_add_fusion.6
  47.1 0.5 fusion.120
  47.6 0.5 fusion.124
  48.1 0.5 fusion.128
  48.6 0.5 fusion.132
  49.2 0.5 fusion.136
  49.7 0.4 fusion.4
  50.1 0.4 fusion.2
  50.4 0.4 fusion.19
  50.8 0.3 fusion.93
  51.2 0.4 fusion.17
  51.6 0.4 fusion.260
  52.0 0.3 fusion.56
  52.3 0.3 fusion.60
  52.6 0.3 fusion.23
  52.9 0.3 fusion.67
  53.2 0.3 convolution_add_fusion.15
  53.4 0.3 fusion.22
  53.7 0.3 fusion.74
  54.0 0.3 convolution_add_fusion.14
  54.3 0.3 fusion.33
  54.6 4.6 %collective-permute-start.7 = (bf16[64,8,128]{2,0,1:T(8,128)(2,1)S(1)}, bf16[64,8,128]{2,0,1:T(8,128)(2,1)S(1)}, u32[]{:S(2)}, u32[]{:S(2)}) collective-permute-start(bf16[64,8,128]{2,0,1:T(8,128)(2,1)S(1)} %fusion.33), channel_id=1, source_target_pairs={{4,0},{8,4},{12,8},{16,12},{20,16},{24,20},{28,24},{5,1},{9,5},{13... | collective-permute-start | bytes 393224 | tf_op jit(solution)/shard_map/ppermute | solution.py:15
  59.4 2.8 %scatter_custom_fusion.1 = f32[64,1024]{0,1:T(8,128)S(1)} fusion(s32[256]{0:T(256)S(1)} %bitcast.272, f32[]{:T(128)} %constant.89.clone.1, bf16[1,64,256]{1,2,0:T(8,128)(2,1)S(1)} %copy.50, pred[256]{0:T(512)(128)(4,1)S(1)} %get-tuple-element.68, bf16[]{:T(256)} %constant.58.clone.2, bf16[1,64,1024]{1,2,0:T(8,128)(2,1)S(1)} %bitcast.261, s32[256]{0:T(256)S(1)} %bitcast.269), kind=kCustom, calls=%fused_computation.118 | custom fusion | flops 81920 | bytes 591366 | tf_op jit(solution)/shard_map/vmap()/scatter-add | solution.py:96
  62.4 0.7 %collective-permute-done.7 = bf16[64,8,128]{2,0,1:T(8,128)(2,1)S(1)} collective-permute-done((bf16[64,8,128]{2,0,1:T(8,128)(2,1)S(1)}, bf16[64,8,128]{2,0,1:T(8,128)(2,1)S(1)}, u32[]{:S(2)}, u32[]{:S(2)}) %collective-permute-start.7) | collective-permute-done | bytes 131104 | tf_op jit(solution)/shard_map/ppermute | solution.py:15
  63.1 0.7 %copy.67 = bf16[1,64,8,128]{3,2,1,0:T(8,128)(2,1)} copy(bf16[1,64,8,128]{3,1,2,0:T(8,128)(2,1)S(1)} %fusion.82) | data formatting | bytes 262144 | tf_op jit(solution)/shard_map/convert_element_type | solution.py:165
  (29 shorter events, 1.8 us)
Async XLA Ops:
  0.0 22.0 %copy-start = (bf16[64,256]{1,0:T(8,128)(2,1)S(1)}, bf16[64,256]{1,0:T(8,128)(2,1)}, u32[]{:S(2)}) copy-start(bf16[64,256]{1,0:T(8,128)(2,1)} %param.15) | copy-start | bytes 98308
  0.9 6.5 %collective-permute-start = (bf16[64,8,128]{2,0,1:T(8,128)(2,1)S(1)}, bf16[64,8,128]{2,0,1:T(8,128)(2,1)S(1)}, u32[]{:S(2)}, u32[]{:S(2)}) collective-permute-start(bf16[64,8,128]{2,0,1:T(8,128)(2,1)S(1)} %bitcast.259), channel_id=1, source_target_pairs={{0,4},{4,8},{8,12},{12,16},{16,20},{20,24},{24,28},{1,5},{5,9},{9,... | collective-permute-start | bytes 393224 | tf_op jit(solution)/shard_map/ppermute | solution.py:15
  7.4 5.3 %collective-permute-start.1 = (bf16[2,64,2,128]{3,1,2,0:T(8,128)(2,1)S(1)}, bf16[2,64,2,128]{3,1,2,0:T(8,128)(2,1)S(1)}, u32[]{:S(2)}, u32[]{:S(2)}) collective-permute-start(bf16[2,64,2,128]{3,1,2,0:T(8,128)(2,1)S(1)} %get-tuple-element.128), channel_id=1, source_target_pairs={{0,1},{1,2},{2,3},{4,5},{5,6},{6,7},{8,9},{9,10},{10,11},{12,13},{... | collective-permute-start | bytes 196616 | tf_op jit(solution)/shard_map/ppermute | solution.py:26
  10.6 5.9 %collective-permute-start.2 = (bf16[2,64,2,128]{3,1,2,0:T(8,128)(2,1)S(1)}, bf16[2,64,2,128]{3,1,2,0:T(8,128)(2,1)S(1)}, u32[]{:S(2)}, u32[]{:S(2)}) collective-permute-start(bf16[2,64,2,128]{3,1,2,0:T(8,128)(2,1)S(1)} %get-tuple-element.130), channel_id=1, source_target_pairs={{1,0},{2,1},{3,2},{5,4},{6,5},{7,6},{9,8},{10,9},{11,10},{13,12},{... | collective-permute-start | bytes 196616 | tf_op jit(solution)/shard_map/ppermute | solution.py:28
  16.8 1.0 %copy-start.1 = (bf16[3,3,256,64]{2,3,1,0:T(8,128)(2,1)S(1)}, bf16[3,3,256,64]{2,3,1,0:T(8,128)(2,1)}, u32[]{:S(2)}) copy-start(bf16[3,3,256,64]{2,3,1,0:T(8,128)(2,1)} %param.13) | copy-start | bytes 884740
  19.3 1.0 %copy-start.4 = (f32[256]{0:T(256)S(1)}, f32[256]{0:T(256)}, u32[]{:S(2)}) copy-start(f32[256]{0:T(256)} %param.14) | copy-start | bytes 3076
  25.5 8.0 %copy-start.2 = (bf16[1,64,8,128]{3,2,1,0:T(8,128)(2,1)S(1)}, bf16[1,64,8,128]{3,2,1,0:T(8,128)(2,1)}, u32[]{:S(2)}) copy-start(bf16[1,64,8,128]{3,2,1,0:T(8,128)(2,1)} %param.9) | copy-start | bytes 393220
  25.5 7.9 %copy-start.3 = (bf16[64,8,128]{2,1,0:T(8,128)(2,1)S(1)}, bf16[64,8,128]{2,1,0:T(8,128)(2,1)}, u32[]{:S(2)}) copy-start(bf16[64,8,128]{2,1,0:T(8,128)(2,1)} %param.10) | copy-start | bytes 393220
  25.8 7.6 %collective-permute-start.3 = (bf16[64,8,128]{2,0,1:T(8,128)(2,1)S(1)}, bf16[64,8,128]{2,0,1:T(8,128)(2,1)S(1)}, u32[]{:S(2)}, u32[]{:S(2)}) collective-permute-start(bf16[64,8,128]{2,0,1:T(8,128)(2,1)S(1)} %fusion.32), channel_id=1, source_target_pairs={{4,0},{8,4},{12,8},{16,12},{20,16},{24,20},{28,24},{5,1},{9,5},{13... | collective-permute-start | bytes 393224 | tf_op jit(solution)/shard_map/ppermute | solution.py:15
  33.6 4.2 %collective-permute-start.4 = (bf16[64,8,128]{2,0,1:T(8,128)(2,1)S(1)}, bf16[64,8,128]{2,0,1:T(8,128)(2,1)S(1)}, u32[]{:S(2)}, u32[]{:S(2)}) collective-permute-start(bf16[64,8,128]{2,0,1:T(8,128)(2,1)S(1)} %bitcast.256), channel_id=1, source_target_pairs={{0,4},{4,8},{8,12},{12,16},{16,20},{20,24},{24,28},{1,5},{5,9},{9,... | collective-permute-start | bytes 393224 | tf_op jit(solution)/shard_map/ppermute | solution.py:15
  37.8 5.5 %collective-permute-start.5 = (bf16[2,64,2,128]{3,1,2,0:T(8,128)(2,1)S(1)}, bf16[2,64,2,128]{3,1,2,0:T(8,128)(2,1)S(1)}, u32[]{:S(2)}, u32[]{:S(2)}) collective-permute-start(bf16[2,64,2,128]{3,1,2,0:T(8,128)(2,1)S(1)} %get-tuple-element.122), channel_id=1, source_target_pairs={{0,1},{1,2},{2,3},{4,5},{5,6},{6,7},{8,9},{9,10},{10,11},{12,13},{... | collective-permute-start | bytes 196616 | tf_op jit(solution)/shard_map/ppermute | solution.py:26
  40.1 5.9 %collective-permute-start.6 = (bf16[2,64,2,128]{3,1,2,0:T(8,128)(2,1)S(1)}, bf16[2,64,2,128]{3,1,2,0:T(8,128)(2,1)S(1)}, u32[]{:S(2)}, u32[]{:S(2)}) collective-permute-start(bf16[2,64,2,128]{3,1,2,0:T(8,128)(2,1)S(1)} %get-tuple-element.123), channel_id=1, source_target_pairs={{1,0},{2,1},{3,2},{5,4},{6,5},{7,6},{9,8},{10,9},{11,10},{13,12},{... | collective-permute-start | bytes 196616 | tf_op jit(solution)/shard_map/ppermute | solution.py:28
  54.6 8.4 %collective-permute-start.7 = (bf16[64,8,128]{2,0,1:T(8,128)(2,1)S(1)}, bf16[64,8,128]{2,0,1:T(8,128)(2,1)S(1)}, u32[]{:S(2)}, u32[]{:S(2)}) collective-permute-start(bf16[64,8,128]{2,0,1:T(8,128)(2,1)S(1)} %fusion.33), channel_id=1, source_target_pairs={{4,0},{8,4},{12,8},{16,12},{20,16},{24,20},{28,24},{5,1},{9,5},{13... | collective-permute-start | bytes 393224 | tf_op jit(solution)/shard_map/ppermute | solution.py:15
where the time goes:
time: 65.2 us; the launch traced here: 63.9 us
  starting transfers between devices  25.2 us (39%)
  matrix products  15 us (23%)
  waiting for transfers between devices  9.81 us (15%)
  local copies, waits for them, and re-layouts  6.85 us (11%)
  other arithmetic  6.54 us (10%)
    ppermute x4, starting transfers between devices, from_behind(): return lax.ppermute(value, axis, pairs)  14.5 us
    dot_general x18, matrix products, advance_one_interval(): jnp.einsum('hc,clm->hlm', input_kernel_weight[row_step, col_step], shift_...  8.38 us
    ppermute x2, waiting for transfers between devices, with_halo(): lax.ppermute(head, axis, [((i + 1) % count, i) for i in range(ends)])  6.36 us
    scatter-add x2, other arithmetic, scatter_one(): jnp.zeros(grid_field.shape, jnp.float32).at[:, column_index].add(misfit)  5.53 us
    ppermute x2, starting transfers between devices, with_halo(): lax.ppermute(head, axis, [((i + 1) % count, i) for i in range(ends)])  5.4 us
    ppermute x2, starting transfers between devices, with_halo(): lax.ppermute(tail, axis, [(i, (i + 1) % count) for i in range(ends)])  5.34 us
    dot_general x18, matrix products, collect_rows(): jnp.einsum('hc,hlm->clm', input_kernel_weight[row_step, col_step], shift_...  5.2 us
    unnamed x13, local copies, waits for them, and re-layouts  3.59 us
  transfers between devices with their start and end apart: 8, of which 5 were waited for; matrix products, arithmetic and copies ran while one was open for 14% of the time, Pallas kernels for 0%

commit v1 on v0

v1 whole, which is shorter than its diff:
```python
import functools

import jax
import jax.numpy as jnp
from jax import lax
from jax.experimental import pallas as pl
from jax.experimental.pallas import tpu as pltpu
from jax.sharding import PartitionSpec as P

ITERS = 2
step_size = 0.3
BF = jnp.bfloat16
F32 = jnp.float32
MESH = pl.DeviceIdType.MESH

TO_LOW, TO_HIGH, TO_PREV, TO_PREV_LOW, TO_PREV_HIGH, FC_MID, FC_LOW, FC_HIGH = range(8)
KINDS = 8


def kernel(
    steps, sub, strips,
    x_hbm, bg_hbm, obs_hbm, idx_hbm, w_hbm, b_hbm, p_hbm,
    out_ref,
    x_in, bg_in, obs_in, idx_in, w_in, b_in, p_in,
    xm, xn, fc, fcin, x3, act, cot, res, part, wf, wt, pt, bias, bgr, osum, ocnt,
    in_sem, send_sem, recv_sem,
):
    t = lax.axis_index("tm")
    l = lax.axis_index("lat")
    chans, height, lon = x_in.shape
    hid = p_in.shape[1]
    has_prev, has_next = t > 0, t < sub - 1
    has_low, has_high = l > 0, l < strips - 1
    t_prev, t_next = lax.rem(t + sub - 1, sub), lax.rem(t + 1, sub)
    l_low, l_high = lax.rem(l + strips - 1, strips), lax.rem(l + 1, strips)
    both = jnp.logical_and

    loads = [
        pltpu.make_async_copy(src, dst, in_sem.at[n])
        for n, (src, dst) in enumerate(
            [(x_hbm, x_in), (w_hbm, w_in), (p_hbm, p_in), (b_hbm, b_in),
             (obs_hbm, obs_in), (idx_hbm, idx_in), (bg_hbm, bg_in)]
        )
    ]
    barrier = pltpu.get_barrier_semaphore()

    def greet(ok, tt, ll):
        @pl.when(ok)
        def _():
            pl.semaphore_signal(barrier, inc=1, device_id=(tt, ll), device_id_type=MESH)

    greet(has_low, t, l_low)
    greet(has_high, t, l_high)
    greet(has_next, t_next, l)
    greet(both(has_next, has_low), t_next, l_low)
    greet(both(has_next, has_high), t_next, l_high)
    greet(has_prev, t_prev, l)
    for load in loads:
        load.start()

    def copies(it):
        own = xm.at[it]
        table = {
            TO_LOW: (own.at[pl.ds(2, 2)], own.at[pl.ds(height + 2, 2)], t, l_low, has_low, has_high),
            TO_HIGH: (own.at[pl.ds(height, 2)], own.at[pl.ds(0, 2)], t, l_high, has_high, has_low),
            TO_PREV: (own.at[pl.ds(2, height)], xn.at[it, pl.ds(1, height)], t_prev, l, has_prev, has_next),
            TO_PREV_LOW: (own.at[pl.ds(2, 1)], xn.at[it, pl.ds(height + 1, 1)], t_prev, l_low,
                          both(has_prev, has_low), both(has_next, has_high)),
            TO_PREV_HIGH: (own.at[pl.ds(height + 1, 1)], xn.at[it, pl.ds(0, 1)], t_prev, l_high,
                           both(has_prev, has_high), both(has_next, has_low)),
            FC_MID: (fc.at[it, pl.ds(2, height - 2)], fcin.at[it, pl.ds(1, height - 2)], t_next, l, has_next, has_prev),
            FC_LOW: (fc.at[it, pl.ds(1, 1)], fcin.at[it, pl.ds(0, 1)], t_next, l, has_next, has_prev),
            FC_HIGH: (fc.at[it, pl.ds(height, 1)], fcin.at[it, pl.ds(height - 1, 1)], t_next, l, has_next, has_prev),
        }
        made = {}
        for kind, (src, dst, tt, ll, sends, receives) in table.items():
            made[kind] = (
                pltpu.make_async_remote_copy(
                    src_ref=src, dst_ref=dst,
                    send_sem=send_sem.at[it, kind], recv_sem=recv_sem.at[it, kind],
                    device_id=(tt, ll), device_id_type=MESH,
                ),
                sends, receives,
            )
        return made

    moves = [copies(it) for it in range(steps)]

    def start(it, kind):
        copy, sends, _ = moves[it][kind]
        pl.when(sends)(lambda: copy.start())

    def arrive(it, kind):
        copy, _, receives = moves[it][kind]
        pl.when(receives)(lambda: copy.wait_recv())

    def left(it, kind):
        copy, sends, _ = moves[it][kind]
        pl.when(sends)(lambda: copy.wait_send())

    def send_state(it):
        for kind in (TO_LOW, TO_HIGH, TO_PREV_LOW, TO_PREV_HIGH, TO_PREV):
            start(it, kind)

    loads[0].wait()
    xm[0, 2 : height + 2] = jnp.swapaxes(x_in[...].astype(F32), 0, 1).astype(BF)
    zero2 = jnp.zeros((2, chans, lon), BF)
    for it in range(steps):
        @pl.when(jnp.logical_not(has_low))
        def _():
            xm[it, 0:2] = zero2
            xn[it, 0:1] = zero2[:1]

        @pl.when(jnp.logical_not(has_high))
        def _():
            xm[it, height + 2 : height + 4] = zero2
            xn[it, height + 1 : height + 2] = zero2[:1]

    one = lambda flag: flag.astype(jnp.int32)
    expected = (
        one(has_low) + one(has_high) + one(has_prev) + one(both(has_prev, has_low))
        + one(both(has_prev, has_high)) + one(has_next)
    )
    pl.semaphore_wait(barrier, expected)
    send_state(0)

    loads[1].wait()
    for a in range(3):
        strip = jnp.concatenate([w_in[a, b] for b in range(3)], axis=1)
        wf[:, a * 3 * chans : (a + 1) * 3 * chans] = strip
        wt[:, a * hid : (a + 1) * hid] = strip.astype(F32).T.astype(BF)
    loads[2].wait()
    pt[...] = p_in[...].astype(F32).T.astype(BF)
    loads[3].wait()
    bias[...] = jnp.broadcast_to(b_in[...], (lon, hid)).T
    loads[4].wait()
    loads[5].wait()
    loads[6].wait()
    obs_n = obs_in.shape[1]
    obs1 = jnp.concatenate([obs_in[...], jnp.ones((16, obs_n), BF)], axis=0)
    local = idx_in[...] - l * (height * lon)
    for r in range(height):
        cells = lax.broadcasted_iota(jnp.int32, (lon, obs_n), 0) + r * lon
        hot = jnp.where(cells == local, 1.0, 0.0).astype(BF)
        both_sums = lax.dot_general(obs1, hot, (((1,), (1,)), ((), ())), preferred_element_type=F32)
        osum[r] = both_sums[:chans]
        ocnt[r] = both_sums[chans : chans + 8]

    @pl.when(jnp.logical_not(has_prev))
    def _():
        bgr[...] = jnp.swapaxes(bg_in[...].astype(F32), 0, 1).astype(BF)

    def fill(it, row):
        v = xm[it, row].astype(F32)
        x3[row, 0:chans] = pltpu.roll(v, 1, 1).astype(BF)
        x3[row, chans : 2 * chans] = xm[it, row]
        x3[row, 2 * chans : 3 * chans] = pltpu.roll(v, lon - 1, 1).astype(BF)

    def forward(it, n):
        rhs = jnp.concatenate(
            [jnp.concatenate([x3[n + a], x3[n + 1 + a]], axis=1) for a in range(3)], axis=0
        )
        before = jnp.dot(wf[...], rhs, preferred_element_type=F32)
        b2 = bias[...]
        active = jnp.tanh(before + jnp.concatenate([b2, b2], axis=1)).astype(BF)
        act[n] = active[:, :lon]
        act[n + 1] = active[:, lon:]
        z = jnp.dot(p_in[...], active, preferred_element_type=F32)
        fc[it, n] = (xm[it, n + 1].astype(F32) + z[:, :lon]).astype(BF)
        fc[it, n + 1] = (xm[it, n + 2].astype(F32) + z[:, lon:]).astype(BF)

    def backward(it, n):
        pair = []
        for r in (n, n + 1):
            mis = (xn[it, r].astype(F32) - fc[it, r].astype(F32)).astype(BF)
            if r == 0:
                mis = jnp.where(has_low, mis, jnp.zeros_like(mis))
            if r == height + 1:
                mis = jnp.where(has_high, mis, jnp.zeros_like(mis))
            res[r] = mis
            pair.append(mis)
        projected = jnp.dot(pt[...], jnp.concatenate(pair, axis=1), preferred_element_type=F32)
        for k, r in enumerate((n, n + 1)):
            a = act[r].astype(F32)
            cot[r] = ((1.0 - a * a) * projected[:, k * lon : (k + 1) * lon]).astype(BF)

    def innovation(it, i):
        x = xm[it, i + 2].astype(F32)
        n = ocnt[i]
        many = jnp.concatenate([n] * (chans // 8), axis=0)
        return x * many - osum[i]

    def spread(it, i):
        rhs = jnp.concatenate(
            [jnp.concatenate([cot[i + 2 - a], cot[i + 3 - a]], axis=1) for a in range(3)], axis=0
        )
        g = jnp.dot(wt[...], rhs, preferred_element_type=F32)
        for k in range(2):
            piece = g[:, k * lon : (k + 1) * lon]
            total = (
                pltpu.roll(piece[:chans], lon - 1, 1)
                + piece[chans : 2 * chans]
                + pltpu.roll(piece[2 * chans :], 1, 1)
            )
            adjoint = (res[i + k + 1].astype(F32) + total).astype(BF).astype(F32)
            part[i + k] = innovation(it, i + k) - adjoint

    for it in range(steps):
        @pl.when(has_next)
        def _():
            for row in range(2, height + 2):
                fill(it, row)
            for n in range(2, height, 2):
                forward(it, n)
        start(it, FC_MID)
        arrive(it, TO_LOW)
        arrive(it, TO_HIGH)

        @pl.when(has_next)
        def _():
            for row in (0, 1, height + 2, height + 3):
                fill(it, row)
            forward(it, 0)
            forward(it, height)
        start(it, FC_LOW)
        start(it, FC_HIGH)
        arrive(it, TO_PREV)
        arrive(it, TO_PREV_LOW)
        arrive(it, TO_PREV_HIGH)

        @pl.when(has_next)
        def _():
            for n in range(0, height + 2, 2):
                backward(it, n)
            for i in range(0, height, 2):
                spread(it, i)

        @pl.when(jnp.logical_not(has_next))
        def _():
            for i in range(height):
                part[i] = innovation(it, i)

        for kind in (FC_MID, FC_LOW, FC_HIGH):
            arrive(it, kind)

        @pl.when(jnp.logical_not(has_prev))
        def _():
            fcin[it] = bgr[...]

        for i in range(height):
            x = xm[it, i + 2].astype(F32)
            mis = (x - fcin[it, i].astype(F32)).astype(BF).astype(F32)
            new = (x - step_size * (mis + part[i])).astype(BF)
            if it + 1 < steps:
                xm[it + 1, i + 2] = new
            else:
                out_ref[i] = new
        if it + 1 < steps:
            send_state(it + 1)

    for it in range(steps):
        for kind in range(KINDS):
            left(it, kind)


def on_device(
    mesh_shape, window_snapshots, background, obs_values, obs_index,
    input_kernel_weight, hidden_bias_vector, output_pointwise_weight,
):
    _, chans, height, lon = window_snapshots.shape
    hid = output_pointwise_weight.shape[1]
    obs_n = obs_values.shape[2]
    vmem = pltpu.VMEM
    anywhere = pl.BlockSpec(memory_space=pl.ANY)
    rows = pl.pallas_call(
        functools.partial(kernel, ITERS, mesh_shape["tm"], mesh_shape["lat"]),
        out_shape=jax.ShapeDtypeStruct((height, chans, lon), BF),
        in_specs=[anywhere] * 7,
        out_specs=pl.BlockSpec(memory_space=pltpu.VMEM),
        scratch_shapes=[
            vmem((chans, height, lon), BF),
            vmem((chans, height, lon), BF),
            vmem((chans, obs_n), BF),
            vmem((1, obs_n), jnp.int32),
            vmem(input_kernel_weight.shape, BF),
            vmem((1, hid), F32),
            vmem((chans, hid), BF),
            vmem((ITERS, height + 4, chans, lon), BF),
            vmem((ITERS, height + 2, chans, lon), BF),
            vmem((ITERS, height + 2, chans, lon), BF),
            vmem((ITERS, height, chans, lon), BF),
            vmem((height + 4, 3 * chans, lon), BF),
            vmem((height + 2, hid, lon), BF),
            vmem((height + 2, hid, lon), BF),
            vmem((height + 2, chans, lon), BF),
            vmem((height, chans, lon), F32),
            vmem((hid, 9 * chans), BF),
            vmem((3 * chans, 3 * hid), BF),
            vmem((hid, chans), BF),
            vmem((hid, lon), F32),
            vmem((height, chans, lon), BF),
            vmem((height, chans, lon), F32),
            vmem((height, 8, lon), F32),
            pltpu.SemaphoreType.DMA((7,)),
            pltpu.SemaphoreType.DMA((ITERS, KINDS)),
            pltpu.SemaphoreType.DMA((ITERS, KINDS)),
        ],
        compiler_params=pltpu.CompilerParams(
            collective_id=0, has_side_effects=True, vmem_limit_bytes=32 * 1024 * 1024
        ),
    )(
        window_snapshots[0], background, obs_values[0], obs_index,
        input_kernel_weight, hidden_bias_vector[None], output_pointwise_weight,
    )
    return jnp.swapaxes(rows, 0, 1)[None]


def solution(mesh):
    placed = (
        P("tm", None, "lat", None),
        P(None, "lat", None),
        P("tm", None, "lat"),
        P("tm", "lat"),
        P(),
        P(),
        P(),
    )
    return jax.shard_map(
        functools.partial(on_device, dict(mesh.shape)),
        mesh=mesh, in_specs=placed, out_specs=P("tm", None, "lat", None), check_vma=False,
    )
```

time: 65.2 us -> 17.2 us (0.26); the launches traced: 63.9 us -> 17.1 us
  starting transfers between devices: 25.2 us -> 0 us
  matrix products: 15 us -> 0 us
  Pallas kernels: 0 us -> 14.9 us
  waiting for transfers between devices: 9.81 us -> 0 us
  other arithmetic: 6.54 us -> 0 us
  local copies, waits for them, and re-layouts: 6.85 us -> 2.1 us
    ppermute x8 -> x0, starting transfers between devices: 25.2 us -> none  [the longest x4 14.5 us: from_behind(): return lax.ppermute(value, axis, pairs)]
    dot_general x40 -> x0, matrix products: 15 us -> none  [the longest x18 8.38 us: advance_one_interval(): jnp.einsum('hc,clm->hlm', input_kernel_weight[row_step, col_step], shift_...]
    pallas_call x0 -> x1, Pallas kernels: none -> 14.9 us  [on_device(): pl.pallas_call(functools.partial(kernel, ITERS, mesh_shape['tm'], mesh_sh...]
    ppermute x8 -> x0, waiting for transfers between devices: 9.81 us -> none  [the longest x2 6.36 us: with_halo(): lax.ppermute(head, axis, [((i + 1) % count, i) for i in range(ends)])]
    scatter-add x2 -> x0, other arithmetic: 5.53 us -> none  [scatter_one(): jnp.zeros(grid_field.shape, jnp.float32).at[:, column_index].add(misfit)]
    unnamed x13, local copies, waits for them, and re-layouts: 3.59 us -> 1.36 us
    slice x8 -> x0, local copies, waits for them, and re-layouts: 1.97 us -> none  [shift_cells(): return jnp.roll(grid_field, offset, axis=grid_field.ndim - 1)]
    broadcast_in_dim x0 -> x1, local copies, waits for them, and re-layouts: none -> 0.74 us  [on_device(): return jnp.swapaxes(rows, 0, 1)[None]]
  transfers between devices with their start and end apart: 8 -> 0, of which waited for: 5 -> 0; matrix products, arithmetic and copies ran while one was open for 14% -> 0% of each run, Pallas kernels for 0% -> 0%
where the time goes in v1:
time: 17.2 us; the launch traced here: 17.1 us
  Pallas kernels  14.9 us (87%)
  local copies, waits for them, and re-layouts  2.1 us (12%)
    pallas_call x1, Pallas kernels, on_device(): pl.pallas_call(functools.partial(kernel, ITERS, mesh_shape['tm'], mesh_sh...  14.9 us
    unnamed x13, local copies, waits for them, and re-layouts  1.36 us
    broadcast_in_dim x1, local copies, waits for them, and re-layouts, on_device(): return jnp.swapaxes(rows, 0, 1)[None]  0.74 us

profile of v1, /device:TPU:19, one launch (start us, length us, event | category | flops | bytes accessed | tf_op | source)
XLA Modules:
  0.0 17.1 jit_solution(8742353160350918433)
XLA Ops:
  0.0 0.0 copy-start
  0.0 0.0 copy-start.1
  0.0 0.0 copy-start.2
  0.0 0.0 copy-start.3
  0.0 0.0 copy-start.4
  0.0 0.0 copy-start.5
  0.0 1.3 %copy.8.w_hbm = bf16[3,3,256,64]{3,2,1,0:T(8,128)(2,1)S(1)} copy(bf16[3,3,256,64]{2,3,1,0:T(8,128)(2,1)} %param.11) | data formatting | bytes 589824 | tf_op args[4]
  1.4 0.0 copy-done
  1.4 0.0 copy-done.1
  1.4 0.0 copy-done.2
  1.4 0.0 copy-done.3
  1.4 0.0 copy-done.4
  1.4 0.0 copy-done.5
  1.4 14.9 %shard_map.73 = bf16[8,64,128]{2,1,0:T(8,128)(2,1)S(1)} custom-call(bf16[64,8,128]{2,1,0:T(8,128)(2,1)S(1)} %bitcast.7, bf16[64,8,128]{2,1,0:T(8,128)(2,1)S(1)} %copy-done.1, bf16[64,256]{1,0:T(8,128)(2,1)S(1)} %bitcast.8, s32[1,256]{1,0:T(1,128)S(1)} %copy-done.4, bf16[3,3,256,64]{3,2,1,0:T(8,128)(2,1)S(1)} %copy.8.w_hbm, f32[1,256]{1,0:T(1,128)S(1)} %bitcast.9, ...), custom_call_target="tpu_custom_call" | custom-call | tf_op jit(solution)/shard_map/pallas_call | solution.py:275
  16.3 0.7 %copy.9 = bf16[1,64,8,128]{3,2,1,0:T(8,128)(2,1)} copy(bf16[1,64,8,128]{3,1,2,0:T(8,128)(2,1)S(1)} %bitcast.6) | data formatting | bytes 262144 | tf_op jit(solution)/shard_map/broadcast_in_dim | solution.py:315
Async XLA Ops:
  0.0 1.4 %copy-start = (bf16[1,64,8,128]{3,2,1,0:T(8,128)(2,1)S(1)}, bf16[1,64,8,128]{3,2,1,0:T(8,128)(2,1)}, u32[]{:S(2)}) copy-start(bf16[1,64,8,128]{3,2,1,0:T(8,128)(2,1)} %param.7) | copy-start | bytes 393220
  0.0 1.4 %copy-start.1 = (bf16[64,8,128]{2,1,0:T(8,128)(2,1)S(1)}, bf16[64,8,128]{2,1,0:T(8,128)(2,1)}, u32[]{:S(2)}) copy-start(bf16[64,8,128]{2,1,0:T(8,128)(2,1)} %bg_hbm.1) | copy-start | bytes 393220
  0.0 1.4 %copy-start.2 = (bf16[1,64,256]{2,1,0:T(8,128)(2,1)S(1)}, bf16[1,64,256]{2,1,0:T(8,128)(2,1)}, u32[]{:S(2)}) copy-start(bf16[1,64,256]{2,1,0:T(8,128)(2,1)} %param.9) | copy-start | bytes 98308
  0.0 1.4 %copy-start.3 = (bf16[64,256]{1,0:T(8,128)(2,1)S(1)}, bf16[64,256]{1,0:T(8,128)(2,1)}, u32[]{:S(2)}) copy-start(bf16[64,256]{1,0:T(8,128)(2,1)} %p_hbm.1) | copy-start | bytes 98308
  0.0 1.4 %copy-start.4 = (s32[1,256]{1,0:T(1,128)S(1)}, s32[1,256]{1,0:T(1,128)}, u32[]{:S(2)}) copy-start(s32[1,256]{1,0:T(1,128)} %idx_hbm.1) | copy-start | bytes 3076
  0.0 1.4 %copy-start.5 = (f32[256]{0:T(256)S(1)}, f32[256]{0:T(256)}, u32[]{:S(2)}) copy-start(f32[256]{0:T(256)} %param.12) | copy-start | bytes 3076

commit v2 on v1

--- a/solution.py
+++ b/solution.py
@@ -126,9 +126,9 @@
 
     loads[1].wait()
     for a in range(3):
-        strip = jnp.concatenate([w_in[a, b] for b in range(3)], axis=1)
-        wf[:, a * 3 * chans : (a + 1) * 3 * chans] = strip
-        wt[:, a * hid : (a + 1) * hid] = strip.astype(F32).T.astype(BF)
+        strip = jnp.concatenate([w_in[a, b] for b in range(3)], axis=0)
+        wt[:, a * hid : (a + 1) * hid] = strip
+        wf[:, a * 3 * chans : (a + 1) * 3 * chans] = strip.astype(F32).T.astype(BF)
     loads[2].wait()
     pt[...] = p_in[...].astype(F32).T.astype(BF)
     loads[3].wait()
@@ -150,37 +150,38 @@
     def _():
         bgr[...] = jnp.swapaxes(bg_in[...].astype(F32), 0, 1).astype(BF)
 
-    def fill(it, row):
-        v = xm[it, row].astype(F32)
-        x3[row, 0:chans] = pltpu.roll(v, 1, 1).astype(BF)
-        x3[row, chans : 2 * chans] = xm[it, row]
-        x3[row, 2 * chans : 3 * chans] = pltpu.roll(v, lon - 1, 1).astype(BF)
-
-    def forward(it, n):
+    def fill(source, target):
+        v = source[...].astype(F32)
+        target[0:chans] = pltpu.roll(v, 1, 1).astype(BF)
+        target[chans : 2 * chans] = source[...]
+        target[2 * chans : 3 * chans] = pltpu.roll(v, lon - 1, 1).astype(BF)
+
+    def hidden(operand, rows):
         rhs = jnp.concatenate(
-            [jnp.concatenate([x3[n + a], x3[n + 1 + a]], axis=1) for a in range(3)], axis=0
+            [jnp.concatenate([operand[r + a] for r in rows], axis=1) for a in range(3)], axis=0
         )
         before = jnp.dot(wf[...], rhs, preferred_element_type=F32)
-        b2 = bias[...]
-        active = jnp.tanh(before + jnp.concatenate([b2, b2], axis=1)).astype(BF)
-        act[n] = active[:, :lon]
-        act[n + 1] = active[:, lon:]
+        return jnp.tanh(before + jnp.concatenate([bias[...]] * len(rows), axis=1)).astype(BF)
+
+    def forward(it, rows):
+        active = hidden(x3, rows)
         z = jnp.dot(p_in[...], active, preferred_element_type=F32)
-        fc[it, n] = (xm[it, n + 1].astype(F32) + z[:, :lon]).astype(BF)
-        fc[it, n + 1] = (xm[it, n + 2].astype(F32) + z[:, lon:]).astype(BF)
-
-    def backward(it, n):
-        pair = []
-        for r in (n, n + 1):
+        for k, r in enumerate(rows):
+            act[r] = active[:, k * lon : (k + 1) * lon]
+            fc[it, r] = (xm[it, r + 1].astype(F32) + z[:, k * lon : (k + 1) * lon]).astype(BF)
+
+    def backward(it, rows):
+        parts = []
+        for r in rows:
             mis = (xn[it, r].astype(F32) - fc[it, r].astype(F32)).astype(BF)
             if r == 0:
                 mis = jnp.where(has_low, mis, jnp.zeros_like(mis))
             if r == height + 1:
                 mis = jnp.where(has_high, mis, jnp.zeros_like(mis))
             res[r] = mis
-            pair.append(mis)
-        projected = jnp.dot(pt[...], jnp.concatenate(pair, axis=1), preferred_element_type=F32)
-        for k, r in enumerate((n, n + 1)):
+            parts.append(mis)
+        projected = jnp.dot(pt[...], jnp.concatenate(parts, axis=1), preferred_element_type=F32)
+        for k, r in enumerate(rows):
             a = act[r].astype(F32)
             cot[r] = ((1.0 - a * a) * projected[:, k * lon : (k + 1) * lon]).astype(BF)
 
@@ -190,28 +191,28 @@
         many = jnp.concatenate([n] * (chans // 8), axis=0)
         return x * many - osum[i]
 
-    def spread(it, i):
+    def spread(it, rows):
         rhs = jnp.concatenate(
-            [jnp.concatenate([cot[i + 2 - a], cot[i + 3 - a]], axis=1) for a in range(3)], axis=0
+            [jnp.concatenate([cot[i + 2 - a] for i in rows], axis=1) for a in range(3)], axis=0
         )
         g = jnp.dot(wt[...], rhs, preferred_element_type=F32)
-        for k in range(2):
+        for k, i in enumerate(rows):
             piece = g[:, k * lon : (k + 1) * lon]
             total = (
                 pltpu.roll(piece[:chans], lon - 1, 1)
                 + piece[chans : 2 * chans]
                 + pltpu.roll(piece[2 * chans :], 1, 1)
             )
-            adjoint = (res[i + k + 1].astype(F32) + total).astype(BF).astype(F32)
-            part[i + k] = innovation(it, i + k) - adjoint
+            adjoint = (res[i + 1].astype(F32) + total).astype(BF).astype(F32)
+            part[i] = innovation(it, i) - adjoint
 
     for it in range(steps):
         @pl.when(has_next)
         def _():
             for row in range(2, height + 2):
-                fill(it, row)
-            for n in range(2, height, 2):
-                forward(it, n)
+                fill(xm.at[it, row], x3.at[row])
+            for rows in [tuple(range(2, height))]:
+                forward(it, rows)
         start(it, FC_MID)
         arrive(it, TO_LOW)
         arrive(it, TO_HIGH)
@@ -219,9 +220,8 @@
         @pl.when(has_next)
         def _():
             for row in (0, 1, height + 2, height + 3):
-                fill(it, row)
-            forward(it, 0)
-            forward(it, height)
+                fill(xm.at[it, row], x3.at[row])
+            forward(it, (0, 1, height, height + 1))
         start(it, FC_LOW)
         start(it, FC_HIGH)
         arrive(it, TO_PREV)
@@ -230,10 +230,10 @@
 
         @pl.when(has_next)
         def _():
-            for n in range(0, height + 2, 2):
-                backward(it, n)
-            for i in range(0, height, 2):
-                spread(it, i)
+            for rows in [tuple(range(height + 2))]:
+                backward(it, rows)
+            for rows in [tuple(range(height))]:
+                spread(it, rows)
 
         @pl.when(jnp.logical_not(has_next))
         def _():
@@ -271,10 +271,10 @@
     hid = output_pointwise_weight.shape[1]
     obs_n = obs_values.shape[2]
     vmem = pltpu.VMEM
-    anywhere = pl.BlockSpec(memory_space=pl.ANY)
+    anywhere = pl.BlockSpec(memory_space=pltpu.HBM)
     rows = pl.pallas_call(
         functools.partial(kernel, ITERS, mesh_shape["tm"], mesh_shape["lat"]),
-        out_shape=jax.ShapeDtypeStruct((height, chans, lon), BF),
+        out_shape=pltpu.VMEM((height, chans, lon), BF),
         in_specs=[anywhere] * 7,
         out_specs=pl.BlockSpec(memory_space=pltpu.VMEM),
         scratch_shapes=[
@@ -282,7 +282,7 @@
             vmem((chans, height, lon), BF),
             vmem((chans, obs_n), BF),
             vmem((1, obs_n), jnp.int32),
-            vmem(input_kernel_weight.shape, BF),
+            vmem((3, 3, chans, hid), BF),
             vmem((1, hid), F32),
             vmem((chans, hid), BF),
             vmem((ITERS, height + 4, chans, lon), BF),
@@ -306,11 +306,11 @@
             pltpu.SemaphoreType.DMA((ITERS, KINDS)),
         ],
         compiler_params=pltpu.CompilerParams(
-            collective_id=0, has_side_effects=True, vmem_limit_bytes=32 * 1024 * 1024
+            collective_id=0, has_side_effects=True, vmem_limit_bytes=60 * 1024 * 1024
         ),
     )(
         window_snapshots[0], background, obs_values[0], obs_index,
-        input_kernel_weight, hidden_bias_vector[None], output_pointwise_weight,
+        jnp.swapaxes(input_kernel_weight, 2, 3), hidden_bias_vector[None], output_pointwise_weight,
     )
     return jnp.swapaxes(rows, 0, 1)[None]
 

time: 17.2 us -> 15.1 us (0.88)
  the two profiles are of different devices: /device:TPU:19 before, /device:TPU:20 now
where the time goes in v2:
time: 15.1 us; the launch traced here: 14.9 us
  Pallas kernels  14.2 us (94%)
  local copies, waits for them, and re-layouts  0.74 us (5%)
    pallas_call x1, Pallas kernels, on_device(): pl.pallas_call(functools.partial(kernel, ITERS, mesh_shape['tm'], mesh_sh...  14.2 us
    broadcast_in_dim x1, local copies, waits for them, and re-layouts, on_device(): return jnp.swapaxes(rows, 0, 1)[None]  0.74 us

profile of v2, /device:TPU:20, one launch (start us, length us, event | category | flops | bytes accessed | tf_op | source)
XLA Modules:
  0.0 14.9 jit_solution(7114155144312047632)
XLA Ops:
  0.0 14.2 %shard_map.73 = bf16[8,64,128]{2,1,0:T(8,128)(2,1)S(1)} custom-call(bf16[64,8,128]{2,1,0:T(8,128)(2,1)} %bitcast.9, bf16[64,8,128]{2,1,0:T(8,128)(2,1)} %bg_hbm.1, bf16[64,256]{1,0:T(8,128)(2,1)} %bitcast.10, s32[1,256]{1,0:T(1,128)} %idx_hbm.1, bf16[3,3,64,256]{3,2,1,0:T(8,128)(2,1)} %bitcast.8, f32[1,256]{1,0:T(1,128)} %bitcast.11, bf16[64,256]{1,0:T(8,128)(2,1)} %p_hbm.1), custom_call_target="tpu_custom_call" | custom-call | tf_op jit(solution)/shard_map/pallas_call | solution.py:275
  14.2 0.7 %copy.8 = bf16[1,64,8,128]{3,2,1,0:T(8,128)(2,1)} copy(bf16[1,64,8,128]{3,1,2,0:T(8,128)(2,1)S(1)} %bitcast.7) | data formatting | bytes 262144 | tf_op jit(solution)/shard_map/broadcast_in_dim | solution.py:315
